TPU v7x, 256 devices: a whole 4x4x8 slice. The times are simulated.
256 devices in a mesh: sub: 64 (over y, z, core), rhs: 4 (over x).
Axes of the slice: x: 4, y: 4, z: 8, core: 2. Of those that a mesh axis runs over, the one named last changes fastest.
Arguments:
- right_side: float32 [256, 252, 512], P('sub', None, 'rhs'), parts along dimension 2, may hold values from -70 to 70
- coupling: bfloat16 [256, 508032], P('sub'), may hold values from -0.0625 to 0.0625
- neighbours: int32 [256, 8], P('sub'), may hold values from 0 to 255, as said below
- inverse: bfloat16 [64, 1512, 1512], P('sub'), may hold values from -1 to 1
- margin: int32 [64, 2], P('sub'), may hold values from 0 to 255, as said below
- counts: int32 [64], P('sub'), may hold values from 1 to 4, as said below
Outputs:
- solution: float32 [256, 252, 512], P('sub', None, 'rhs'), parts along dimension 2
There are 4 independent parts, one for each index of `rhs`. A program takes and returns all parts, laid end to end along the dimension named above; an argument that names none is the same for every part. Nothing has to cross between parts.
Inputs may be any that keep to these rules, and one draw needn't show every extreme that they name: `counts`: every subdomain holds 1 to 4 live spheres, and some subdomain holds exactly 4. `neighbours`: every entry of row i is a live sphere slot of the subdomain of i or of a subdomain adjacent to it (index one lower or one higher). `margin`: for subdomain d the first 1 entries are live slots of subdomain d - 1 (of subdomain 0 itself for d = 0), the last 1 live slots of subdomain d + 1 (of the last subdomain itself for the last one).
All inputs are finite; a program needn't handle non-finite values.
Results may differ from a plain program's by a relative error of at most 0.0055.
Values may be sent and summed in bfloat16 or wider, within the bound.
No kernel may reach another device: no remote copies, remote signals or barrier semaphores. Data moves between devices by JAX's collectives and lax.ppermute only.
A program may use at most 64 MiB of HBM per device.

v0:
```python
import jax
import jax.numpy as jnp
from jax import lax
from jax.sharding import PartitionSpec as P

epsilon = 1e-06


def extended_2(block, sides, width):
    for axis, dim in sides:
        count = lax.axis_size(axis)
        forward = [(i, i + 1) for i in range(count - 1)]
        backward = [(target, source) for source, target in forward]
        low = lax.ppermute(
            lax.slice_in_dim(block, block.shape[dim] - width, None, axis=dim), axis, forward
        )
        high = lax.ppermute(lax.slice_in_dim(block, 0, width, axis=dim), axis, backward)
        block = jnp.concatenate([low, block, high], axis=dim)
    return block


def passed_along(x, axis, by):
    size = lax.axis_size(axis)
    pairs = [(i, i + by) for i in range(size) if 0 <= i + by < size]
    return lax.ppermute(x, axis, pairs)


def inner(left, right):
    return jnp.sum(left * right, axis=(0, 1))


def global_norm(vector):
    return jnp.sqrt(lax.psum(inner(vector, vector), "sub") + epsilon)


def body(right_side, coupling, neighbours, inverse, margin, counts):
    rows = right_side.shape[0]
    width = right_side.shape[1]
    fields = right_side.shape[2]
    blocks = neighbours.shape[1]
    matrices = coupling.reshape(rows, blocks, width, width)
    here = lax.axis_index("sub")
    slots = jnp.arange(rows, dtype=jnp.int32)
    alive = (slots < counts[0]).astype(jnp.float32)[:, None, None]
    offset = (here - 1) * rows
    frame_slots = jnp.arange(3 * rows, dtype=jnp.int32)
    extra_slots = margin[0]
    picker = (extra_slots[:, None] - offset == frame_slots[None, :]).astype(jnp.float32)
    picker_low = picker.astype(jnp.bfloat16)
    near_local = (neighbours - offset).reshape(-1)

    def precondition(vector):
        rounded = vector.astype(jnp.bfloat16)
        frame = extended_2(rounded, (("sub", 0),), rows)
        extra = jnp.einsum(
            "hq,qwr->hwr", picker_low, frame, preferred_element_type=jnp.float32
        ).astype(jnp.bfloat16)
        extended = jnp.concatenate([rounded, extra], axis=0).reshape(-1, fields)
        output = jnp.dot(inverse[0], extended, preferred_element_type=jnp.float32)
        output = output.reshape(-1, width, fields)
        spill = output[rows:]
        framed = jnp.einsum("hq,hwr->qwr", picker, spill, precision=lax.Precision.HIGHEST)
        from_right = passed_along(framed[:rows].astype(jnp.bfloat16), "sub", -1).astype(jnp.float32)
        from_left = passed_along(framed[2 * rows :].astype(jnp.bfloat16), "sub", 1).astype(
            jnp.float32
        )
        result = output[:rows] + framed[rows : 2 * rows] + from_right + from_left
        return result * alive

    def apply_system(vector):
        rounded = vector.astype(jnp.bfloat16)
        frame = extended_2(rounded, (("sub", 0),), rows)
        nearby = jnp.take(frame, near_local, axis=0).reshape(rows, blocks, width, fields)
        product = jnp.einsum("pkvw,pkwr->pvr", matrices, nearby, preferred_element_type=jnp.float32)
        return (vector + product) * alive

    start = right_side * alive
    initial = global_norm(start)
    basis_one = start / initial[None, None, :]
    pre_one = precondition(basis_one)
    image = apply_system(pre_one)
    h_one_one = lax.psum(inner(basis_one, image), "sub")
    image = image - h_one_one[None, None, :] * basis_one
    h_two_one = global_norm(image)
    basis_two = image / h_two_one[None, None, :]
    pre_two = precondition(basis_two)
    image = apply_system(pre_two)
    h_one_two = lax.psum(inner(basis_one, image), "sub")
    image = image - h_one_two[None, None, :] * basis_one
    h_two_two = lax.psum(inner(basis_two, image), "sub")
    image = image - h_two_two[None, None, :] * basis_two
    h_three_two = global_norm(image)
    gram_aa = h_one_one * h_one_one + h_two_one * h_two_one
    gram_ab = h_one_one * h_one_two + h_two_one * h_two_two
    gram_bb = h_one_two * h_one_two + h_two_two * h_two_two + h_three_two * h_three_two
    determinant = gram_aa * gram_bb - gram_ab * gram_ab
    weight_one = initial * (gram_bb * h_one_one - gram_ab * h_one_two) / determinant
    weight_two = initial * (gram_aa * h_one_two - gram_ab * h_one_one) / determinant
    return weight_one[None, None, :] * pre_one + weight_two[None, None, :] * pre_two


def solution(mesh):
    placed = (
        P("sub", None, "rhs"),
        P("sub", None),
        P("sub", None),
        P("sub", None, None),
        P("sub", None),
        P("sub"),
    )
    return jax.shard_map(
        body, mesh=mesh, in_specs=placed, out_specs=P("sub", None, "rhs"), check_vma=False
    )
```

profile of v0, /device:TPU:1, one launch (start us, length us, event | category | flops | bytes accessed | tf_op | source)
XLA Modules:
  0.0 864.6 jit_solution(13683966303049429386)
XLA Ops:
  0.7 1.4 multiply_reduce_fusion.5
  2.1 128.3 %psum.42 = f32[128]{0:T(128)S(1)} all-reduce(f32[128]{0:T(128)S(1)} %multiply_reduce_fusion.5), channel_id=1, replica_groups=mesh['sub'=64,'rhs'=4] {'sub'}, use_global_device_ids=true, to_apply=%region_1.0 | all-reduce | flops 128 | bytes 1024 | tf_op jit(solution)/shard_map/psum | solution.py:33
  130.3 1.2 fusion.48
  131.6 6.9 collective-permute-start.1
  138.5 1.9 collective-permute-start
  141.1 2.6 collective-permute-done
  144.7 3.7 fusion.4
  149.2 2.2 fusion.51
  151.3 0.9 fusion.50
  152.3 1.9 collective-permute-start.2
  154.2 4.4 collective-permute-start.3
  159.5 1.1 slice.47
  161.0 1.2 collective-permute-done.3
  162.2 2.4 fusion.46
  164.6 1.9 collective-permute-start.5
  166.5 4.6 collective-permute-start.4
  171.1 6.9 reshape.82
  178.0 13.2 %reshape.53 = bf16[4,8,252,252]{3,2,1,0:T(8,128)(2,1)} reshape(bf16[2032128]{0:T(1024)(128)(2,1)} %reshape.82) | data formatting | bytes 8128512 | tf_op jit(solution)/shard_map/reshape | solution.py:41
  192.0 1.0 gather_fusion
  193.2 1.9 copy-done
  195.1 1.2 convolution_bitcast_fusion.1
  196.9 121.4 %psum.43 = f32[128]{0:T(128)S(1)} all-reduce(f32[128]{0:T(128)S(1)} %get-tuple-element.12), channel_id=1, replica_groups=mesh['sub'=64,'rhs'=4] {'sub'}, use_global_device_ids=true, to_apply=%region_3.5 | all-reduce | flops 128 | bytes 1024 | tf_op jit(solution)/shard_map/psum | solution.py:82
  318.6 126.5 %psum.44 = f32[128]{0:T(128)S(1)} all-reduce(f32[128]{0:T(128)S(1)} %multiply_reduce_fusion.3), channel_id=1, replica_groups=mesh['sub'=64,'rhs'=4] {'sub'}, use_global_device_ids=true, to_apply=%region_5.7 | all-reduce | flops 128 | bytes 1024 | tf_op jit(solution)/shard_map/psum | solution.py:33
  445.1 1.0 fusion.44
  446.1 2.5 collective-permute-start.7
  448.6 3.0 collective-permute-start.6
  451.7 2.1 collective-permute-done.7
  453.7 1.2 collective-permute-done.6
  455.9 3.7 fusion.7
  460.4 2.2 fusion.52
  462.6 0.9 fusion.49
  463.5 1.9 collective-permute-start.8
  465.4 4.4 collective-permute-start.9
  469.8 0.9 slice.69
  470.7 1.1 slice.54
  472.2 1.2 collective-permute-done.9
  473.4 2.5 fusion.42
  475.8 1.9 collective-permute-start.11
  477.7 4.4 collective-permute-start.10
  482.1 2.1 collective-permute-done.11
  484.2 1.2 collective-permute-done.10
  486.1 1.0 gather_fusion.1
  487.4 1.9 copy-done.1
  489.3 1.2 convolution_bitcast_fusion
  491.1 120.7 %psum.45 = f32[128]{0:T(128)S(1)} all-reduce(f32[128]{0:T(128)S(1)} %get-tuple-element.6), channel_id=1, replica_groups=mesh['sub'=64,'rhs'=4] {'sub'}, use_global_device_ids=true, to_apply=%region_7.9 | all-reduce | flops 128 | bytes 1024 | tf_op jit(solution)/shard_map/psum | solution.py:88
  612.1 127.2 %psum.46 = f32[128]{0:T(128)S(1)} all-reduce(f32[128]{0:T(128)S(1)} %multiply_reduce_fusion.1), channel_id=1, replica_groups=mesh['sub'=64,'rhs'=4] {'sub'}, use_global_device_ids=true, to_apply=%region_9.11 | all-reduce | flops 128 | bytes 1024 | tf_op jit(solution)/shard_map/psum | solution.py:90
  739.6 124.0 %psum.47 = f32[128]{0:T(128)S(1)} all-reduce(f32[128]{0:T(128)S(1)} %multiply_reduce_fusion), channel_id=1, replica_groups=mesh['sub'=64,'rhs'=4] {'sub'}, use_global_device_ids=true, to_apply=%region_11.13 | all-reduce | flops 128 | bytes 1024 | tf_op jit(solution)/shard_map/psum | solution.py:33
  863.7 0.9 multiply_add_fusion
  (51 shorter events, 9.8 us)
Async XLA Ops:
  131.6 9.5 %collective-permute-start.1 = (bf16[4,252,128]{2,0,1:T(4,128)(2,1)S(1)}, bf16[4,252,128]{2,0,1:T(4,128)(2,1)S(1)}, u32[]{:S(2)}, u32[]{:S(2)}) collective-permute-start(bf16[4,252,128]{2,0,1:T(4,128)(2,1)S(1)} %get-tuple-element.16), channel_id=1, source_target_pairs={{4,0},{8,4},{12,8},{16,12},{20,16},{24,20},{28,24},{32,28},{36,32}... | collective-permute-start | bytes 774152 | tf_op jit(solution)/shard_map/ppermute | solution.py:17
  138.5 5.2 collective-permute-start
  149.2 9.4 %copy-start.6 = (s32[4,8]{1,0:T(4,128)S(1)}, s32[4,8]{1,0:T(4,128)}, u32[]{:S(2)}) copy-start(s32[4,8]{1,0:T(4,128)} %param.10) | copy-start | bytes 388
  152.3 8.7 %collective-permute-start.2 = (bf16[4,252,128]{2,0,1:T(4,128)(2,1)}, bf16[4,252,128]{2,0,1:T(4,128)(2,1)}, u32[]{:S(2)}, u32[]{:S(2)}) collective-permute-start(bf16[4,252,128]{2,0,1:T(4,128)(2,1)} %get-tuple-element.20), channel_id=1, source_target_pairs={{4,0},{8,4},{12,8},{16,12},{20,16},{24,20},{28,24},{32,28},{36,32}... | collective-permute-start | bytes 774152 | tf_op jit(solution)/shard_map/ppermute | solution.py:25
  154.2 8.0 collective-permute-start.3
  164.6 26.6 %collective-permute-start.5 = (bf16[4,252,128]{2,0,1:T(4,128)(2,1)S(1)}, bf16[4,252,128]{2,0,1:T(4,128)(2,1)S(1)}, u32[]{:S(2)}, u32[]{:S(2)}) collective-permute-start(bf16[4,252,128]{2,0,1:T(4,128)(2,1)S(1)} %get-tuple-element.14), channel_id=1, source_target_pairs={{4,0},{8,4},{12,8},{16,12},{20,16},{24,20},{28,24},{32,28},{36,32}... | collective-permute-start | bytes 774152 | tf_op jit(solution)/shard_map/ppermute | solution.py:17
  166.5 24.7 %collective-permute-start.4 = (bf16[4,252,128]{2,0,1:T(4,128)(2,1)S(1)}, bf16[4,252,128]{2,0,1:T(4,128)(2,1)S(1)}, u32[]{:S(2)}, u32[]{:S(2)}) collective-permute-start(bf16[4,252,128]{2,0,1:T(4,128)(2,1)S(1)} %get-tuple-element.14), channel_id=1, source_target_pairs={{0,4},{4,8},{8,12},{12,16},{16,20},{20,24},{24,28},{28,32},{32,36}... | collective-permute-start | bytes 774152 | tf_op jit(solution)/shard_map/ppermute | solution.py:14
  192.9 2.2 copy-start
  195.1 1.3 copy-start.2
  446.1 7.6 collective-permute-start.7
  448.6 6.3 collective-permute-start.6
  463.5 8.7 %collective-permute-start.8 = (bf16[4,252,128]{2,0,1:T(4,128)(2,1)}, bf16[4,252,128]{2,0,1:T(4,128)(2,1)}, u32[]{:S(2)}, u32[]{:S(2)}) collective-permute-start(bf16[4,252,128]{2,0,1:T(4,128)(2,1)} %get-tuple-element.18), channel_id=1, source_target_pairs={{4,0},{8,4},{12,8},{16,12},{20,16},{24,20},{28,24},{32,28},{36,32}... | collective-permute-start | bytes 774152 | tf_op jit(solution)/shard_map/ppermute | solution.py:25
  465.4 8.0 collective-permute-start.9
  475.8 8.4 collective-permute-start.11
  477.7 7.6 collective-permute-start.10
  487.1 2.2 copy-start.1
  489.3 1.3 copy-start.4
  490.5 121.2 %copy-start.5 = (f32[4,252,128]{2,0,1:T(4,128)S(1)}, f32[4,252,128]{2,0,1:T(4,128)}, u32[]{:S(2)}) copy-start(f32[4,252,128]{2,0,1:T(4,128)} %get-tuple-element.11) | copy-start | bytes 1548292
  490.5 373.1 %copy-start.3 = (f32[4,252,128]{2,0,1:T(4,128)S(1)}, f32[4,252,128]{2,0,1:T(4,128)}, u32[]{:S(2)}) copy-start(f32[4,252,128]{2,0,1:T(4,128)} %get-tuple-element.15) | copy-start | bytes 1548292
where the time goes:
time: 866 us; the launch traced here: 865 us
  blocking collectives  748 us (86%)
  starting transfers between devices  39.8 us (5%)
  local copies, waits for them, and re-layouts  33.8 us (4%)
  matrix products  15.4 us (2%)
  other arithmetic  14.1 us (2%)
  waiting for transfers between devices  12.3 us (1%)
    psum x3, blocking collectives, global_norm(): return jnp.sqrt(lax.psum(inner(vector, vector), 'sub') + epsilon)  379 us
    psum x1, blocking collectives, body(): h_two_two = lax.psum(inner(basis_two, image), 'sub')  127 us
    psum x1, blocking collectives, body(): h_one_one = lax.psum(inner(basis_one, image), 'sub')  121 us
    psum x1, blocking collectives, body(): h_one_two = lax.psum(inner(basis_one, image), 'sub')  121 us
  transfers between devices with their start and end apart: 12, of which 9 were waited for; matrix products, arithmetic and copies ran while one was open for 3% of the time, Pallas kernels for 0%

commit v1 on v0

--- a/solution.py
+++ b/solution.py
@@ -79,7 +79,7 @@
     basis_one = start / initial[None, None, :]
     pre_one = precondition(basis_one)
     image = apply_system(pre_one)
-    h_one_one = lax.psum(inner(basis_one, image), "sub")
+    h_one_one = jnp.sum(lax.all_gather(inner(basis_one, image), "sub"), axis=0)
     image = image - h_one_one[None, None, :] * basis_one
     h_two_one = global_norm(image)
     basis_two = image / h_two_one[None, None, :]

time: 866 us -> 779 us (0.90)
  blocking collectives: 748 us -> 660 us
    psum x1 -> x0, blocking collectives: 121 us -> none  [body(): h_one_one = lax.psum(inner(basis_one, image), 'sub')]
    all_gather x0 -> x1, blocking collectives: none -> 36.1 us  [body(): h_one_one = jnp.sum(lax.all_gather(inner(basis_one, image), 'sub'), axis=0)]
where the time goes in v1:
time: 779 us; the launch traced here: 778 us
  blocking collectives  660 us (85%)
  starting transfers between devices  41.2 us (5%)
  local copies, waits for them, and re-layouts  33.8 us (4%)
  matrix products  15.4 us (2%)
  other arithmetic  14.2 us (2%)
  waiting for transfers between devices  12 us (2%)
    psum x3, blocking collectives, global_norm(): return jnp.sqrt(lax.psum(inner(vector, vector), 'sub') + epsilon)  376 us
    psum x1, blocking collectives, body(): h_two_two = lax.psum(inner(basis_two, image), 'sub')  127 us
    psum x1, blocking collectives, body(): h_one_two = lax.psum(inner(basis_one, image), 'sub')  121 us
    all_gather x1, blocking collectives, body(): h_one_one = jnp.sum(lax.all_gather(inner(basis_one, image), 'sub'), axis=0)  36.1 us
  transfers between devices with their start and end apart: 12, of which 9 were waited for; matrix products, arithmetic and copies ran while one was open for 3% of the time, Pallas kernels for 0%

profile of v1, /device:TPU:1, one launch (start us, length us, event | category | flops | bytes accessed | tf_op | source)
XLA Modules:
  0.0 777.6 jit_solution(6537542247033549400)
XLA Ops:
  0.7 1.4 multiply_reduce_fusion.5
  2.1 128.3 %psum.35 = f32[128]{0:T(128)S(1)} all-reduce(f32[128]{0:T(128)S(1)} %multiply_reduce_fusion.5), channel_id=1, replica_groups=mesh['sub'=64,'rhs'=4] {'sub'}, use_global_device_ids=true, to_apply=%region_1.0 | all-reduce | flops 128 | bytes 1024 | tf_op jit(solution)/shard_map/psum | solution.py:33
  130.3 1.2 fusion.48
  131.6 6.9 collective-permute-start.1
  138.5 1.9 collective-permute-start
  141.1 2.6 collective-permute-done
  144.7 3.7 fusion.4
  149.2 2.2 fusion.51
  151.3 0.9 fusion.50
  152.3 1.9 collective-permute-start.2
  154.2 4.4 collective-permute-start.3
  159.5 1.1 slice.47
  161.0 1.2 collective-permute-done.3
  162.2 2.4 fusion.46
  164.6 1.9 collective-permute-start.5
  166.5 4.6 collective-permute-start.4
  171.1 6.9 reshape.86
  178.0 13.2 %reshape.53 = bf16[4,8,252,252]{3,2,1,0:T(8,128)(2,1)} reshape(bf16[2032128]{0:T(1024)(128)(2,1)} %reshape.86) | data formatting | bytes 8128512 | tf_op jit(solution)/shard_map/reshape | solution.py:41
  192.0 1.0 gather_fusion
  193.2 1.9 copy-done
  195.1 1.2 convolution_bitcast_fusion.1
  196.9 36.1 %all-gather.1 = f32[64,1,128]{2,1,0:T(1,128)S(1)} all-gather(f32[1,1,128]{2,1,0:T(1,128)S(1)} %bitcast.55), channel_id=2, replica_groups=mesh['sub'=64,'rhs'=4] {'sub'}, dimensions={0}, use_global_device_ids=true | all-gather | bytes 33280 | tf_op jit(solution)/shard_map/all_gather | solution.py:82
  233.3 123.6 %psum.36 = f32[128]{0:T(128)S(1)} all-reduce(f32[128]{0:T(128)S(1)} %multiply_reduce_fusion.3), channel_id=1, replica_groups=mesh['sub'=64,'rhs'=4] {'sub'}, use_global_device_ids=true, to_apply=%region_5.7 | all-reduce | flops 128 | bytes 1024 | tf_op jit(solution)/shard_map/psum | solution.py:33
  356.9 1.0 fusion.44
  357.9 4.8 collective-permute-start.7
  362.7 1.9 collective-permute-start.6
  364.6 0.9 collective-permute-done.7
  365.5 2.4 collective-permute-done.6
  368.9 3.7 fusion.7
  373.4 2.2 fusion.52
  375.5 0.9 fusion.49
  376.5 1.9 collective-permute-start.8
  378.4 4.4 collective-permute-start.9
  382.8 0.9 slice.69
  383.6 1.1 slice.54
  385.2 1.2 collective-permute-done.9
  386.3 2.5 fusion.42
  388.8 1.9 collective-permute-start.11
  390.7 4.6 collective-permute-start.10
  395.4 1.8 collective-permute-done.11
  397.2 1.2 collective-permute-done.10
  399.1 1.0 gather_fusion.1
  400.3 1.9 copy-done.1
  402.2 1.2 convolution_bitcast_fusion
  404.0 120.7 %psum.37 = f32[128]{0:T(128)S(1)} all-reduce(f32[128]{0:T(128)S(1)} %get-tuple-element.6), channel_id=1, replica_groups=mesh['sub'=64,'rhs'=4] {'sub'}, use_global_device_ids=true, to_apply=%region_7.9 | all-reduce | flops 128 | bytes 1024 | tf_op jit(solution)/shard_map/psum | solution.py:88
  525.0 127.2 %psum.38 = f32[128]{0:T(128)S(1)} all-reduce(f32[128]{0:T(128)S(1)} %multiply_reduce_fusion.1), channel_id=1, replica_groups=mesh['sub'=64,'rhs'=4] {'sub'}, use_global_device_ids=true, to_apply=%region_9.11 | all-reduce | flops 128 | bytes 1024 | tf_op jit(solution)/shard_map/psum | solution.py:90
  652.6 124.0 %psum.39 = f32[128]{0:T(128)S(1)} all-reduce(f32[128]{0:T(128)S(1)} %multiply_reduce_fusion), channel_id=1, replica_groups=mesh['sub'=64,'rhs'=4] {'sub'}, use_global_device_ids=true, to_apply=%region_11.13 | all-reduce | flops 128 | bytes 1024 | tf_op jit(solution)/shard_map/psum | solution.py:33
  776.7 0.9 multiply_add_fusion
  (52 shorter events, 9.9 us)
Async XLA Ops:
  131.6 9.5 %collective-permute-start.1 = (bf16[4,252,128]{2,0,1:T(4,128)(2,1)S(1)}, bf16[4,252,128]{2,0,1:T(4,128)(2,1)S(1)}, u32[]{:S(2)}, u32[]{:S(2)}) collective-permute-start(bf16[4,252,128]{2,0,1:T(4,128)(2,1)S(1)} %get-tuple-element.16), channel_id=1, source_target_pairs={{4,0},{8,4},{12,8},{16,12},{20,16},{24,20},{28,24},{32,28},{36,32}... | collective-permute-start | bytes 774152 | tf_op jit(solution)/shard_map/ppermute | solution.py:17
  138.5 5.2 collective-permute-start
  149.2 9.4 %copy-start.6 = (s32[4,8]{1,0:T(4,128)S(1)}, s32[4,8]{1,0:T(4,128)}, u32[]{:S(2)}) copy-start(s32[4,8]{1,0:T(4,128)} %param.10) | copy-start | bytes 388
  152.3 8.7 %collective-permute-start.2 = (bf16[4,252,128]{2,0,1:T(4,128)(2,1)}, bf16[4,252,128]{2,0,1:T(4,128)(2,1)}, u32[]{:S(2)}, u32[]{:S(2)}) collective-permute-start(bf16[4,252,128]{2,0,1:T(4,128)(2,1)} %get-tuple-element.20), channel_id=1, source_target_pairs={{4,0},{8,4},{12,8},{16,12},{20,16},{24,20},{28,24},{32,28},{36,32}... | collective-permute-start | bytes 774152 | tf_op jit(solution)/shard_map/ppermute | solution.py:25
  154.2 8.0 %collective-permute-start.3 = (bf16[4,252,128]{2,0,1:T(4,128)(2,1)}, bf16[4,252,128]{2,0,1:T(4,128)(2,1)}, u32[]{:S(2)}, u32[]{:S(2)}) collective-permute-start(bf16[4,252,128]{2,0,1:T(4,128)(2,1)} %get-tuple-element.21), channel_id=1, source_target_pairs={{0,4},{4,8},{8,12},{12,16},{16,20},{20,24},{24,28},{28,32},{32,36}... | collective-permute-start | bytes 774152 | tf_op jit(solution)/shard_map/ppermute | solution.py:25
  164.6 26.6 %collective-permute-start.5 = (bf16[4,252,128]{2,0,1:T(4,128)(2,1)S(1)}, bf16[4,252,128]{2,0,1:T(4,128)(2,1)S(1)}, u32[]{:S(2)}, u32[]{:S(2)}) collective-permute-start(bf16[4,252,128]{2,0,1:T(4,128)(2,1)S(1)} %get-tuple-element.14), channel_id=1, source_target_pairs={{4,0},{8,4},{12,8},{16,12},{20,16},{24,20},{28,24},{32,28},{36,32}... | collective-permute-start | bytes 774152 | tf_op jit(solution)/shard_map/ppermute | solution.py:17
  166.5 24.7 %collective-permute-start.4 = (bf16[4,252,128]{2,0,1:T(4,128)(2,1)S(1)}, bf16[4,252,128]{2,0,1:T(4,128)(2,1)S(1)}, u32[]{:S(2)}, u32[]{:S(2)}) collective-permute-start(bf16[4,252,128]{2,0,1:T(4,128)(2,1)S(1)} %get-tuple-element.14), channel_id=1, source_target_pairs={{0,4},{4,8},{8,12},{12,16},{16,20},{20,24},{24,28},{28,32},{32,36}... | collective-permute-start | bytes 774152 | tf_op jit(solution)/shard_map/ppermute | solution.py:14
  192.9 2.2 copy-start
  195.1 1.3 copy-start.2
  357.9 7.6 collective-permute-start.7
  362.7 5.2 collective-permute-start.6
  376.5 8.7 %collective-permute-start.8 = (bf16[4,252,128]{2,0,1:T(4,128)(2,1)}, bf16[4,252,128]{2,0,1:T(4,128)(2,1)}, u32[]{:S(2)}, u32[]{:S(2)}) collective-permute-start(bf16[4,252,128]{2,0,1:T(4,128)(2,1)} %get-tuple-element.18), channel_id=1, source_target_pairs={{4,0},{8,4},{12,8},{16,12},{20,16},{24,20},{28,24},{32,28},{36,32}... | collective-permute-start | bytes 774152 | tf_op jit(solution)/shard_map/ppermute | solution.py:25
  378.4 8.0 %collective-permute-start.9 = (bf16[4,252,128]{2,0,1:T(4,128)(2,1)}, bf16[4,252,128]{2,0,1:T(4,128)(2,1)}, u32[]{:S(2)}, u32[]{:S(2)}) collective-permute-start(bf16[4,252,128]{2,0,1:T(4,128)(2,1)} %get-tuple-element.19), channel_id=1, source_target_pairs={{0,4},{4,8},{8,12},{12,16},{16,20},{20,24},{24,28},{28,32},{32,36}... | collective-permute-start | bytes 774152 | tf_op jit(solution)/shard_map/ppermute | solution.py:25
  388.8 8.4 %collective-permute-start.11 = (bf16[4,252,128]{2,0,1:T(4,128)(2,1)S(1)}, bf16[4,252,128]{2,0,1:T(4,128)(2,1)S(1)}, u32[]{:S(2)}, u32[]{:S(2)}) collective-permute-start(bf16[4,252,128]{2,0,1:T(4,128)(2,1)S(1)} %get-tuple-element.8), channel_id=1, source_target_pairs={{4,0},{8,4},{12,8},{16,12},{20,16},{24,20},{28,24},{32,28},{36,32}... | collective-permute-start | bytes 774152 | tf_op jit(solution)/shard_map/ppermute | solution.py:17
  390.7 7.6 collective-permute-start.10
  400.1 2.2 copy-start.1
  402.2 1.3 copy-start.4
  403.5 121.2 %copy-start.5 = (f32[4,252,128]{2,0,1:T(4,128)S(1)}, f32[4,252,128]{2,0,1:T(4,128)}, u32[]{:S(2)}) copy-start(f32[4,252,128]{2,0,1:T(4,128)} %get-tuple-element.11) | copy-start | bytes 1548292
  403.5 373.1 %copy-start.3 = (f32[4,252,128]{2,0,1:T(4,128)S(1)}, f32[4,252,128]{2,0,1:T(4,128)}, u32[]{:S(2)}) copy-start(f32[4,252,128]{2,0,1:T(4,128)} %get-tuple-element.15) | copy-start | bytes 1548292
